TPU v7x, 512 devices: a whole 4x4x16 slice. The times are simulated.
512 devices in a mesh: leaf: 128 (over y, z, core), rhs: 4 (over x).
Axes of the slice: x: 4, y: 4, z: 16, core: 2. Of those that a mesh axis runs over, the one named last changes fastest.
Arguments:
- leaf_rhs: bfloat16 [262144, 512], P('leaf', 'rhs'), may hold values from -6 to 6
- leaf_inverse: bfloat16 [2048, 128, 128], P('leaf'), as said below
- panels: bfloat16 [2048, 4, 128, 128], P('leaf'), may hold values from -0.02734375 to 0.02734375
- ancestors: int32 [2048, 4], P('leaf'), may hold values from 0 to 7, as said below
- pattern: int32 [2048, 4], P('leaf'), may hold values 0 or 1
- top_rhs: bfloat16 [1024, 512], P(None, 'rhs'), may hold values from -6 to 6
- top_inverse: bfloat16 [4, 256, 256], P('rhs'), as said below
Outputs:
- leaf_solution: float32 [262144, 512], P('leaf', 'rhs')
- top_solution: bfloat16 [1024, 512], P(None, 'rhs')
Inputs may be any that keep to these rules, and one draw needn't show every extreme that they name: `ancestors`: each leaf's 4 entries are distinct row blocks, consecutive modulo 8. `leaf_inverse`: lower triangular with a diagonal of positive entries. `top_inverse`: lower triangular with a diagonal of positive entries.
All inputs are finite; a program needn't handle non-finite values. No bound on the sum of `pattern` on one device may be relied on, other than what follows from the above.
Results may differ from a plain program's by a relative error of at most 0.014.
Values may be sent and summed in bfloat16 or wider, within the bound.
A program may use at most 64 MiB of HBM per device.

v0:
```python
import jax
import jax.numpy as jnp
from jax import lax
from jax.sharding import PartitionSpec as P


def solve_tops(inverses, reduced):
    top_count, top_width, _ = inverses.shape
    col_count = reduced.shape[1]
    shaped = reduced.reshape(top_count, top_width, col_count)
    middle = jnp.einsum(
        "tij,tjc->tic", inverses, shaped, preferred_element_type=jnp.float32
    ).astype(jnp.bfloat16)
    result = jnp.einsum(
        "tji,tjc->tic", inverses, middle, preferred_element_type=jnp.float32
    ).astype(jnp.bfloat16)
    return result.reshape(top_count * top_width, col_count)


def shards(leaf_rhs, leaf_inverse, panels, ancestors, pattern, top_rhs, top_inverse):
    leaf_count, width, _ = leaf_inverse.shape
    col_count = leaf_rhs.shape[1]
    blk_rows = panels.shape[2]
    top_rows = top_rhs.shape[0]
    block_count = top_rows // blk_rows
    rhs_blocks = leaf_rhs.reshape(leaf_count, width, col_count)
    solved = jnp.einsum(
        "lij,ljc->lic", leaf_inverse, rhs_blocks, preferred_element_type=jnp.float32
    ).astype(jnp.bfloat16)
    select = (
        ancestors[:, :, None] == jnp.arange(block_count, dtype=jnp.int32)[None, None, :]
    ).astype(jnp.float32)
    select = select * pattern[:, :, None].astype(jnp.float32)
    terms = jnp.einsum("lkpj,ljc->lkpc", panels, solved, preferred_element_type=jnp.float32)
    update = jnp.einsum("lkb,lkpc->bpc", select, terms).reshape(top_rows, col_count)
    update_sum = lax.psum(update, "leaf")
    reduced = (top_rhs.astype(jnp.float32) - update_sum).astype(jnp.bfloat16)
    inverses = lax.all_gather(top_inverse, "rhs", axis=0, tiled=True)
    top_solution = solve_tops(inverses, reduced)
    known = top_solution.reshape(block_count, blk_rows, col_count).astype(jnp.float32)
    gathered = jnp.einsum("lkb,bpc->lkpc", select, known).astype(jnp.bfloat16)
    back_sum = jnp.einsum("lkpj,lkpc->ljc", panels, gathered, preferred_element_type=jnp.float32)
    remainder = (solved.astype(jnp.float32) - back_sum).astype(jnp.bfloat16)
    leaf_solution = jnp.einsum(
        "lji,ljc->lic", leaf_inverse, remainder, preferred_element_type=jnp.float32
    )
    return (leaf_solution.reshape(leaf_count * width, col_count), top_solution)


def solution(mesh):
    placed = (
        P("leaf", "rhs"),
        P("leaf", None, None),
        P("leaf", None, None, None),
        P("leaf", None),
        P("leaf", None),
        P(None, "rhs"),
        P("rhs", None, None),
    )
    return jax.shard_map(
        shards,
        mesh=mesh,
        in_specs=placed,
        out_specs=(P("leaf", "rhs"), P(None, "rhs")),
        check_vma=False,
    )
```

profile of v0, /device:TPU:1, one launch (start us, length us, event | category | flops | bytes accessed | tf_op | source)
XLA Modules:
  0.0 371.2 jit_solution(10551160909385808623)
XLA Ops:
  7.2 0.0 copy-start
  7.2 0.0 all-reduce.2.cloned.1.call-start
  7.2 1.6 convolution_convert_fusion.1
  8.9 0.2 copy-done
  9.1 2.1 convolution_bitcast_fusion
  11.2 0.0 copy-start.5
  11.2 0.0 copy-start.4
  11.2 4.6 %copy.15 = bf16[16,4,128,128]{3,0,1,2:T(8,128)(2,1)} copy(bf16[16,4,128,128]{2,3,1,0:T(8,128)(2,1)} %convolution_bitcast_fusion) | data formatting | bytes 4194304 | tf_op jit(solution)/shard_map/lkpj,ljc->lkpc/dot_general | solution.py:34
  15.8 0.0 copy-done.5
  15.8 0.0 copy-done.4
  15.8 0.0 copy-start.3
  15.8 2.2 convolution_bitcast_fusion.1
  18.0 0.9 copy.16
  18.9 0.0 all-reduce.2.cloned.1.call-update
  18.9 0.0 copy-done.3
  19.0 11.1 %all_gather.3 = bf16[4,256,256]{2,1,0:T(8,128)(2,1)S(1)} all-gather(bf16[1,256,256]{2,1,0:T(8,128)(2,1)S(1)} %copy-done.3), channel_id=1, replica_groups=mesh['leaf'=128,'rhs'=4] {'rhs'}, dimensions={0}, use_global_device_ids=true | all-gather | bytes 655360 | tf_op jit(solution)/shard_map/all_gather | solution.py:38
  30.0 324.2 %all-reduce.2.cloned.1.call-done = f32[1024,128]{1,0:T(8,128)} async-done(((f32[1024,128]{1,0:T(8,128)}), f32[1024,128]{1,0:T(8,128)}) %all-reduce.2.cloned.1.call-update) | async-done | bytes 524304 | tf_op jit(solution)/shard_map/psum | solution.py:36
  354.3 1.2 subtract_convert_fusion
  355.4 1.1 fusion.14
  356.6 0.0 copy-start.1
  356.6 1.2 copy.18
  357.8 0.0 copy-start.2
  357.8 2.1 convolution_convert_fusion
  359.9 0.0 copy-done.1
  359.9 4.5 %fusion.12 = f32[16,128,128]{1,2,0:T(8,128)} fusion(bf16[16,128,128]{2,1,0:T(8,128)(2,1)S(1)} %copy-done.1, bf16[16,4,128,128]{3,2,1,0:T(8,128)(2,1)S(1)} %copy-done, bf16[16,4,128,128]{3,0,2,1:T(8,128)(2,1)} %convolution_convert_fusion, bf16[16,128,128]{2,1,0:T(8,128)(2,1)S(1)} %convolution_convert_fusion.1), kind=kOutput, calls=%fused_computation.9 | convolution fusion | flops 336330752 | bytes 6291456 | tf_op jit(solution)/shard_map/lji,ljc->lic/dot_general | solution.py:44
  364.4 0.0 copy-done.2
  (1 shorter events, 0.0 us)
Async XLA Ops:
  7.2 1.9 copy-start
  7.2 347.1 %all-reduce.2.cloned.1.call-start = ((), (), s32[]{:S(2)}) async-start(), calls=%async_computation | async-start | bytes 1048576 | tf_op jit(solution)/shard_map/psum | solution.py:36
  11.2 4.6 %copy-start.5 = (s32[16,4]{0,1:T(4,128)S(1)}, s32[16,4]{0,1:T(4,128)}, u32[]{:S(2)}) copy-start(s32[16,4]{0,1:T(4,128)} %param.11) | copy-start | bytes 772
  11.2 4.6 %copy-start.4 = (s32[16,4]{0,1:T(4,128)S(1)}, s32[16,4]{0,1:T(4,128)}, u32[]{:S(2)}) copy-start(s32[16,4]{0,1:T(4,128)} %param.10) | copy-start | bytes 772
  15.8 3.2 copy-start.3
  356.6 3.3 copy-start.1
  357.8 6.6 %copy-start.2 = (bf16[4,256,128]{2,1,0:T(8,128)(2,1)}, bf16[4,256,128]{2,1,0:T(8,128)(2,1)S(1)}, u32[]{:S(2)}) copy-start(bf16[4,256,128]{2,1,0:T(8,128)(2,1)S(1)} %copy.18) | copy-start | bytes 786436
Sparse Core Ops, SparseCore 0:
  19.1 335.1 all-reduce.1
where the time goes:
time: 372 us; the launch traced here: 371 us
  waiting for transfers between devices  324 us (87%)
  between operations  14.1 us (4%)
  matrix products  13.7 us (4%)
  blocking collectives  11.1 us (3%)
  local copies, waits for them, and re-layouts  6.9 us (2%)
    psum x1, waiting for transfers between devices, shards(): update_sum = lax.psum(update, 'leaf')  324 us
    all_gather x1, blocking collectives, shards(): inverses = lax.all_gather(top_inverse, 'rhs', axis=0, tiled=True)  11.1 us
  transfers between devices with their start and end apart: 1, of which 1 were waited for; matrix products, arithmetic and copies ran while one was open for 0% of the time, Pallas kernels for 0%

commit v1 on v0

v1 whole, which is shorter than its diff:
```python
import functools
import jax
import jax.numpy as jnp
from jax import lax
from jax.experimental import pallas as pl
from jax.experimental.pallas import tpu as pltpu
from jax.sharding import PartitionSpec as P

MESH = pl.DeviceIdType.MESH
BF = jnp.bfloat16
F32 = jnp.float32
NY, NZ = 4, 16
LV = 16
NB = 8


def place():
    leaf = lax.axis_index("leaf")
    return leaf // (2 * NZ), (leaf // 2) % NZ, leaf % 2, lax.axis_index("rhs")


def device(y, z, c, x):
    return ((y * NZ + z) * 2 + c, x)


def send(src, dst, send_sem, recv_sem, to):
    pltpu.make_async_remote_copy(
        src_ref=src, dst_ref=dst, send_sem=send_sem, recv_sem=recv_sem, device_id=to, device_id_type=MESH
    ).start()


def take(like, sem):
    pltpu.make_async_copy(like, like, sem).wait()


def forward_kernel(
    rhs_h, inv_h, pan_h, anc, pat, trhs_h, tinv_h, s_out, x_out,
    rhs, inv, pan, solved, acc, own, half_tx, half_rx, tx1, rx1, tx2, rx2, trhs, red, tops, xs,
    in_sem, out_sem, half_s, half_r, s1_s, s1_r, s2_s, s2_r, s3_s, s3_r, s4_s, s4_r, t_s, t_r,
):
    y, z, c, x = place()
    zr, za = z % 4, z // 4
    grp = y * 4 + zr
    bar = pltpu.get_barrier_semaphore()

    def greet(to):
        pl.semaphore_signal(bar, inc=1, device_id=to, device_id_type=MESH)

    greet(device(y, z, 1 - c, x))
    for dy in range(4):
        for d in (-2, -1, 0, 1):
            if (dy, d) != (0, 0):
                greet(device((y - dy) % 4, (z - d) % NZ, c, x))
    for k in (1, 2, 3):
        greet(device(y, (z + 4 * k) % NZ, c, x))
        greet(device(y, z, c, (x + k) % 4))

    loads = [
        pltpu.make_async_copy(rhs_h, rhs, in_sem.at[0]),
        pltpu.make_async_copy(inv_h, inv, in_sem.at[1]),
        pltpu.make_async_copy(pan_h, pan.at[:, pl.ds(0, 4)], in_sem.at[2]),
        pltpu.make_async_copy(tinv_h.at[0], tops.at[x], in_sem.at[3]),
        pltpu.make_async_copy(
            trhs_h.at[pl.ds(pl.multiple_of((grp // 2) * 128 + c * 64 + (grp % 2) * 32, 32), 32)], trhs, in_sem.at[4]
        ),
    ]
    for load in loads:
        load.start()
    pan[:, 4] = jnp.zeros((LV, 128, 128), BF)
    loads[0].wait()
    loads[1].wait()

    def solve(l, _):
        rows = pl.ds(pl.multiple_of(l * 128, 128), 128)
        solved[rows] = jnp.dot(inv[l], rhs[rows], preferred_element_type=F32).astype(BF)
        return 0

    lax.fori_loop(0, LV, solve, 0, unroll=4)
    s_copy = pltpu.make_async_copy(solved, s_out, out_sem.at[0])
    s_copy.start()
    loads[2].wait()
    loads[3].wait()
    pl.semaphore_wait(bar, 22)
    for k in (1, 2, 3):
        send(tops.at[x], tops.at[x], t_s, t_r, device(y, z, c, (x + k) % 4))

    def spread(i):
        to_y = (y + 1 + i // 2) % 4
        dy = (1 + i // 2) % 4
        take(half_rx.at[i], half_r.at[i])
        tx1[i] = (own[i] + half_rx[i].astype(F32)).astype(BF)
        for h in range(2):
            r = 2 * (i % 2) + h
            d = (r - z + 2) % 4
            slot = dy * 4 + d
            piece = tx1.at[i, pl.ds(h * 32, 32)]
            mine = (dy == 0) & (d == 2)

            @pl.when(jnp.logical_not(mine))
            def _():
                send(piece, rx1.at[slot], s1_s, s1_r, device(to_y, (z + d - 2) % NZ, c, x))

            @pl.when(mine)
            def _():
                rx1[2] = piece[...]

    def block(i, _):
        b = 2 * ((y + 1 + i // 2) % 4) + i % 2
        parts = []
        for l in range(LV):
            kk = 4
            for k in range(4):
                kk = jnp.where((anc[l, k] == b) & (pat[l, k] != 0), k, kk)
            parts.append(pan[l, kk])
        acc[...] = jnp.dot(jnp.concatenate(parts, axis=1), solved[...], preferred_element_type=F32)
        half_tx[i] = acc[pl.ds(pl.multiple_of((1 - c) * 64, 64), 64)].astype(BF)
        send(half_tx.at[i], half_rx.at[i], half_s, half_r.at[i], device(y, z, 1 - c, x))
        own[i] = acc[pl.ds(pl.multiple_of(c * 64, 64), 64)]

        @pl.when(i > 0)
        def _():
            spread(i - 1)

        return 0

    lax.fori_loop(0, NB, block, 0)
    spread(NB - 1)

    take(rx1.at[pl.ds(0, 15)], s1_r)
    total = rx1[0].astype(F32)
    for slot in range(1, 16):
        total = total + rx1[slot].astype(F32)
    tx2[...] = total.astype(BF)
    for k in (2, 1, 3):
        send(tx2, rx2.at[za], s2_s, s2_r, device(y, (z + 4 * k) % NZ, c, x))
    rx2[za] = tx2[...]
    loads[4].wait()
    take(rx2.at[pl.ds(0, 3)], s2_r)
    total = rx2[0].astype(F32)
    for k in range(1, 4):
        total = total + rx2[k].astype(F32)
    red[c, grp] = (trhs[...].astype(F32) - total).astype(BF)
    piece = red.at[c, grp]
    for dy in (2, 1, 3, 0):
        for d in (-2, 1, -1, 0):
            if (dy, d) != (0, 0):
                send(piece, piece, s3_s, s3_r.at[dy], device((y + dy) % 4, (z + d) % NZ, c, x))
    for dy in (0, 1, 3, 2):
        from_y = (y - dy) % 4
        quarter = red.at[c, pl.ds(pl.multiple_of(from_y * 4, 4), 4)]
        take(red.at[c, pl.ds(0, 3 if dy == 0 else 4)], s3_r.at[dy])
        send(quarter, quarter, s4_s, s4_r.at[dy], device(y, z, 1 - c, x))
    take(tops.at[pl.ds(0, 3)], t_r)
    for dy in (0, 1, 3, 2):
        t = (y - dy) % 4
        take(red.at[c, pl.ds(0, 4)], s4_r.at[dy])
        parts = []
        for j in range(2):
            for core in range(2):
                for h in range(2):
                    parts.append(red[core, t * 4 + 2 * j + h])
        reduced = jnp.concatenate(parts, axis=0)
        middle = jnp.dot(tops[t], reduced, preferred_element_type=F32).astype(BF)
        xs[t] = lax.dot_general(tops[t], middle, (((0,), (0,)), ((), ())), preferred_element_type=F32).astype(BF)
    x_copy = pltpu.make_async_copy(xs, x_out, out_sem.at[1])
    x_copy.start()
    take(half_tx, half_s)
    take(rx1.at[pl.ds(0, 15)], s1_s)
    take(rx2.at[pl.ds(0, 3)], s2_s)
    take(rx1.at[pl.ds(0, 15)], s3_s)
    take(red.at[c], s4_s)
    take(tops.at[pl.ds(0, 3)], t_s)
    s_copy.wait()
    x_copy.wait()


def backward_kernel(inv, pan, solved, xs, anc, pat, out, x_out, known):
    known[pl.ds(0, NB)] = xs[...]
    known[NB] = jnp.zeros((128, 128), BF)
    x_out[...] = xs[...]
    for l in range(LV):
        parts = []
        for k in range(4):
            parts.append(known[jnp.where(pat[l, k] != 0, anc[l, k], NB)])
        back = lax.dot_general(
            pan[l].reshape(512, 128), jnp.concatenate(parts, axis=0), (((0,), (0,)), ((), ())), preferred_element_type=F32
        )
        rem = (solved[l].astype(F32) - back).astype(BF)
        out[l] = lax.dot_general(inv[l], rem, (((0,), (0,)), ((), ())), preferred_element_type=F32)


def shards(leaf_rhs, leaf_inverse, panels, ancestors, pattern, top_rhs, top_inverse):
    any_spec = pl.BlockSpec(memory_space=pl.ANY)
    smem = pl.BlockSpec(memory_space=pltpu.SMEM)
    vmem = pl.BlockSpec(memory_space=pltpu.VMEM)
    V, D = pltpu.VMEM, pltpu.SemaphoreType.DMA
    solved, xs = pl.pallas_call(
        forward_kernel,
        out_shape=(jax.ShapeDtypeStruct((2048, 128), BF), jax.ShapeDtypeStruct((4, 256, 128), BF)),
        in_specs=[any_spec, any_spec, any_spec, smem, smem, any_spec, any_spec],
        out_specs=(any_spec, any_spec),
        scratch_shapes=[
            V((2048, 128), BF), V((LV, 128, 128), BF), V((LV, 5, 128, 128), BF), V((2048, 128), BF),
            V((128, 128), F32), V((NB, 64, 128), F32), V((NB, 64, 128), BF), V((NB, 64, 128), BF),
            V((NB, 64, 128), BF), V((16, 32, 128), BF), V((32, 128), BF), V((4, 32, 128), BF),
            V((32, 128), BF), V((2, 16, 32, 128), BF), V((4, 256, 256), BF), V((4, 256, 128), BF),
            D((5,)), D((2,)), D, D((NB,)), D, D, D, D, D, D((4,)), D, D((4,)), D, D,
        ],
        compiler_params=pltpu.CompilerParams(collective_id=0, has_side_effects=True, vmem_limit_bytes=24 * 2**20),
        cost_estimate=pl.CostEstimate(flops=700_000_000, bytes_accessed=4_000_000, transcendentals=0),
        name="forward",
    )(leaf_rhs, leaf_inverse, panels, ancestors, pattern, top_rhs, top_inverse)
    leaf_solution, top_solution = pl.pallas_call(
        backward_kernel,
        out_shape=(jax.ShapeDtypeStruct((LV, 128, 128), F32), jax.ShapeDtypeStruct((NB, 128, 128), BF)),
        in_specs=[vmem, vmem, vmem, vmem, smem, smem],
        out_specs=(vmem, vmem),
        scratch_shapes=[V((NB + 1, 128, 128), BF)],
        compiler_params=pltpu.CompilerParams(vmem_limit_bytes=24 * 2**20),
        cost_estimate=pl.CostEstimate(flops=400_000_000, bytes_accessed=4_000_000, transcendentals=0),
        name="backward",
    )(leaf_inverse, panels, solved.reshape(LV, 128, 128), xs.reshape(NB, 128, 128), ancestors, pattern)
    return leaf_solution.reshape(LV * 128, 128), top_solution.reshape(NB * 128, 128)


def solution(mesh):
    placed = (
        P("leaf", "rhs"),
        P("leaf", None, None),
        P("leaf", None, None, None),
        P("leaf", None),
        P("leaf", None),
        P(None, "rhs"),
        P("rhs", None, None),
    )
    return jax.shard_map(
        shards, mesh=mesh, in_specs=placed, out_specs=(P("leaf", "rhs"), P(None, "rhs")), check_vma=False
    )
```

time: 372 us -> 52.5 us (0.14)
  waiting for transfers between devices: 324 us -> 0 us
  Pallas kernels: 0 us -> 44.4 us
  matrix products: 13.7 us -> 0 us
  between operations: 14.1 us -> 0.65 us
  blocking collectives: 11.1 us -> 0 us
    psum x1 -> x0, waiting for transfers between devices: 324 us -> none  [shards(): update_sum = lax.psum(update, 'leaf')]
    pallas_call x0 -> x2, Pallas kernels: none -> 44.4 us  [the longest x1 39.7 us: shards(): pl.pallas_call(forward_kernel, out_shape=(jax.ShapeDtypeStruct((2048, 128...]
    dot_general x6 -> x0, matrix products: 13.7 us -> none  [the longest x1 4.48 us: shards(): jnp.einsum('lji,ljc->lic', leaf_inverse, remainder, preferred_element_typ...]
    all_gather x1 -> x0, blocking collectives: 11.1 us -> none  [shards(): inverses = lax.all_gather(top_inverse, 'rhs', axis=0, tiled=True)]
    unnamed x12 -> x14, local copies, waits for them, and re-layouts: 0.24 us -> 7.05 us
    dot_general x2 -> x0, local copies, waits for them, and re-layouts: 5.48 us -> none  [the longest x1 4.58 us: shards(): jnp.einsum('lkpj,ljc->lkpc', panels, solved, preferred_element_type=jnp.f...]
  transfers between devices with their start and end apart: 1 -> 0, of which waited for: 1 -> 0; matrix products, arithmetic and copies ran while one was open for 0% -> 0% of each run, Pallas kernels for 0% -> 0%
where the time goes in v1:
time: 52.5 us; the launch traced here: 52.1 us
  Pallas kernels  44.4 us (85%)
  local copies, waits for them, and re-layouts  7.05 us (13%)
  between operations  0.65 us (1%)
    pallas_call x1, Pallas kernels, shards(): pl.pallas_call(forward_kernel, out_shape=(jax.ShapeDtypeStruct((2048, 128...  39.7 us
    unnamed x14, local copies, waits for them, and re-layouts  7.05 us
    pallas_call x1, Pallas kernels, shards(): pl.pallas_call(backward_kernel, out_shape=(jax.ShapeDtypeStruct((LV, 128,...  4.71 us

profile of v1, /device:TPU:1, one launch (start us, length us, event | category | flops | bytes accessed | tf_op | source)
XLA Modules:
  0.0 52.1 jit_solution(3652761228190870228)
XLA Ops:
  0.6 0.8 %copy.9.anc = s32[16,4]{1,0:T(8,128)S(1)} copy(s32[16,4]{0,1:T(4,128)} %param.10) | data formatting | bytes 512 | tf_op args[3]
  1.4 0.8 %copy.10.pat = s32[16,4]{1,0:T(8,128)S(1)} copy(s32[16,4]{0,1:T(4,128)} %param.11) | data formatting | bytes 512 | tf_op args[4]
  2.1 0.0 copy-start
  2.1 1.6 %copy-done = bf16[16,4,128,128]{3,2,1,0:T(8,128)(2,1)S(1)} copy-done((bf16[16,4,128,128]{3,2,1,0:T(8,128)(2,1)S(1)}, bf16[16,4,128,128]{3,2,1,0:T(8,128)(2,1)}, u32[]{:S(2)}) %copy-start) | copy-done | bytes 2097176
  3.7 0.0 copy-start.2
  3.7 1.0 %copy-done.2 = bf16[16,128,128]{2,1,0:T(8,128)(2,1)S(1)} copy-done((bf16[16,128,128]{2,1,0:T(8,128)(2,1)S(1)}, bf16[16,128,128]{2,1,0:T(8,128)(2,1)}, u32[]{:S(2)}) %copy-start.2) | copy-done | bytes 524312
  4.8 0.0 copy-start.3
  4.8 1.0 %copy-done.3 = bf16[2048,128]{1,0:T(8,128)(2,1)S(1)} copy-done((bf16[2048,128]{1,0:T(8,128)(2,1)S(1)}, bf16[2048,128]{1,0:T(8,128)(2,1)}, u32[]{:S(2)}) %copy-start.3) | copy-done | bytes 524312
  5.8 0.0 copy-start.4
  5.8 0.9 %copy-done.4 = bf16[1024,128]{1,0:T(8,128)(2,1)S(1)} copy-done((bf16[1024,128]{1,0:T(8,128)(2,1)S(1)}, bf16[1024,128]{1,0:T(8,128)(2,1)}, u32[]{:S(2)}) %copy-start.4) | copy-done | bytes 262168
  6.8 0.0 copy-start.5
  6.8 0.9 %copy-done.5 = bf16[1,256,256]{2,1,0:T(8,128)(2,1)S(1)} copy-done((bf16[1,256,256]{2,1,0:T(8,128)(2,1)S(1)}, bf16[1,256,256]{2,1,0:T(8,128)(2,1)}, u32[]{:S(2)}) %copy-start.5) | copy-done | bytes 131096
  7.7 0.0 copy-start.1
  7.7 39.7 %forward.1 = (bf16[2048,128]{1,0:T(8,128)(2,1)S(1)}, bf16[4,256,128]{2,1,0:T(8,128)(2,1)S(1)}) custom-call(bf16[2048,128]{1,0:T(8,128)(2,1)S(1)} %copy-done.3, bf16[16,128,128]{2,1,0:T(8,128)(2,1)S(1)} %copy-done.2, bf16[16,4,128,128]{3,2,1,0:T(8,128)(2,1)S(1)} %copy-done, s32[16,4]{1,0:T(8,128)S(1)} %copy.9.anc, s32[16,4]{1,0:T(8,128)S(1)} %copy.10.pat, ...), custom_call_target="tpu_custom_call" | custom-call | flops 700000000 | bytes 4000000 | tf_op jit(solution)/shard_map/forward/pallas_call | solution.py:197
  47.4 0.0 copy-done.1
  47.4 4.7 %backward.1 = (f32[16,128,128]{2,1,0:T(8,128)}, bf16[8,128,128]{2,1,0:T(8,128)(2,1)}) custom-call(bf16[16,128,128]{2,1,0:T(8,128)(2,1)S(1)} %copy-done.2, bf16[16,4,128,128]{3,2,1,0:T(8,128)(2,1)S(1)} %copy-done.1, bf16[16,128,128]{2,1,0:T(8,128)(2,1)S(1)} %bitcast.4, bf16[8,128,128]{2,1,0:T(8,128)(2,1)S(1)} %bitcast.5, s32[16,4]{1,0:T(8,128)S(1)} %copy.9.anc, ...), custom_call_target="tpu_custom_call" | custom-call | flops 400000000 | bytes 4000000 | tf_op jit(solution)/shard_map/backward/pallas_call | solution.py:213
Async XLA Ops:
  2.1 1.6 %copy-start = (bf16[16,4,128,128]{3,2,1,0:T(8,128)(2,1)S(1)}, bf16[16,4,128,128]{3,2,1,0:T(8,128)(2,1)}, u32[]{:S(2)}) copy-start(bf16[16,4,128,128]{3,2,1,0:T(8,128)(2,1)} %pan.1) | copy-start | bytes 6291460
  3.7 1.0 %copy-start.2 = (bf16[16,128,128]{2,1,0:T(8,128)(2,1)S(1)}, bf16[16,128,128]{2,1,0:T(8,128)(2,1)}, u32[]{:S(2)}) copy-start(bf16[16,128,128]{2,1,0:T(8,128)(2,1)} %inv.1) | copy-start | bytes 1572868
  4.8 1.0 %copy-start.3 = (bf16[2048,128]{1,0:T(8,128)(2,1)S(1)}, bf16[2048,128]{1,0:T(8,128)(2,1)}, u32[]{:S(2)}) copy-start(bf16[2048,128]{1,0:T(8,128)(2,1)} %rhs_h.1) | copy-start | bytes 1572868
  5.8 0.9 %copy-start.4 = (bf16[1024,128]{1,0:T(8,128)(2,1)S(1)}, bf16[1024,128]{1,0:T(8,128)(2,1)}, u32[]{:S(2)}) copy-start(bf16[1024,128]{1,0:T(8,128)(2,1)} %trhs_h.1) | copy-start | bytes 786436
  6.8 0.9 %copy-start.5 = (bf16[1,256,256]{2,1,0:T(8,128)(2,1)S(1)}, bf16[1,256,256]{2,1,0:T(8,128)(2,1)}, u32[]{:S(2)}) copy-start(bf16[1,256,256]{2,1,0:T(8,128)(2,1)} %tinv_h.1) | copy-start | bytes 393220
  7.7 39.7 %copy-start.1 = (bf16[16,4,128,128]{3,2,1,0:T(8,128)(2,1)S(1)}, bf16[16,4,128,128]{3,2,1,0:T(8,128)(2,1)}, u32[]{:S(2)}) copy-start(bf16[16,4,128,128]{3,2,1,0:T(8,128)(2,1)} %pan.1) | copy-start | bytes 6291460

commit v2 on v1

v2 whole, which is shorter than its diff:
```python
import functools
import jax
import jax.numpy as jnp
from jax import lax
from jax.experimental import pallas as pl
from jax.experimental.pallas import tpu as pltpu
from jax.sharding import PartitionSpec as P

MESH = pl.DeviceIdType.MESH
BF = jnp.bfloat16
F32 = jnp.float32
NY, NZ = 4, 16
LV = 16
NB = 8
CHAIN = True
TSEND = True
ORDER = (2, 1, 3, 0)
PER = 2


def place():
    leaf = lax.axis_index("leaf")
    return leaf // (2 * NZ), (leaf // 2) % NZ, leaf % 2, lax.axis_index("rhs")


def device(y, z, c, x):
    return ((y * NZ + z) * 2 + c, x)


def send(src, dst, send_sem, recv_sem, to):
    pltpu.make_async_remote_copy(
        src_ref=src, dst_ref=dst, send_sem=send_sem, recv_sem=recv_sem, device_id=to, device_id_type=MESH
    ).start()


def take(like, sem):
    pltpu.make_async_copy(like, like, sem).wait()


def forward_kernel(
    rhs_h, inv_h, pan_h, anc_h, pat_h, trhs_h, tinv_h, solved_o, flip_o, invt_o, tops_o, topt_o, red_o,
    rhs, inv, pan, anc, pat, which, solved, flip, invt, tops, topt,
    half_tx, half_rx, tx1, rx1, tx2, rx2, trhs, mine_red,
    in_sem, out_sem, near, far, half_s, half_r, s1_s, s1_r, s2_s, s2_r, s3_s, s3_r, s4_s, s4_r, t_s, t_r,
):
    y, z, c, x = place()
    zr, za = z % 4, z // 4
    grp = y * 4 + zr
    bar = pltpu.get_barrier_semaphore()

    loads = [
        pltpu.make_async_copy(anc_h, anc, in_sem.at[0]),
        pltpu.make_async_copy(pat_h, pat, in_sem.at[1]),
        pltpu.make_async_copy(rhs_h, rhs, in_sem.at[2]),
        pltpu.make_async_copy(inv_h, inv, in_sem.at[3]),
        pltpu.make_async_copy(pan_h, pan.at[:, pl.ds(0, 4)], in_sem.at[4]),
        pltpu.make_async_copy(
            trhs_h.at[pl.ds(pl.multiple_of((grp // 2) * 128 + c * 64 + (grp % 2) * 32, 32), 32)], trhs, in_sem.at[5]
        ),
        pltpu.make_async_copy(tinv_h.at[0], tops.at[x], in_sem.at[6]),
    ]
    for load in loads:
        load.start()

    def signal(sem, to):
        pl.semaphore_signal(sem, inc=1, device_id=to, device_id_type=MESH)

    for dy in (2, 1, 3, 0):
        for d in (-2, 2, -1, 1, 0):
            if (dy, d) != (0, 0) and (d != 2 or dy == 0):
                signal(bar, device((y - dy) % 4, (z - d) % NZ, c, x))
    for k in (2, 1, 3):
        signal(bar, device(y, z, c, (x + k) % 4))
    signal(bar, device(y, z, 1 - c, x))
    if not CHAIN:
        for k in (2, 1, 3):
            signal(bar, device(y, (z + 4 * k) % NZ, c, x))

    pan[:, 4] = jnp.zeros((LV, 128, 128), BF)
    loads[0].wait()
    loads[1].wait()
    for l in range(LV):
        stored = [jnp.where(pat[k, l] != 0, k, 4) for k in range(4)]
        blocks = [anc[k, l] for k in range(4)]
        for b in range(NB):
            kk = 4
            for k in range(4):
                kk = jnp.where(blocks[k] == b, stored[k], kk)
            which[b, l] = kk
    loads[2].wait()
    loads[3].wait()
    for l in range(LV):
        rows = pl.ds(l * 128, 128)
        solved[rows] = jnp.dot(inv[l], rhs[rows], preferred_element_type=F32).astype(BF)
    outs = [
        pltpu.make_async_copy(solved, solved_o, out_sem.at[0]),
        pltpu.make_async_copy(flip, flip_o, out_sem.at[1]),
        pltpu.make_async_copy(invt, invt_o, out_sem.at[2]),
        pltpu.make_async_copy(mine_red, red_o.at[c, grp], out_sem.at[3]),
        pltpu.make_async_copy(tops, tops_o, out_sem.at[4]),
        pltpu.make_async_copy(topt, topt_o, out_sem.at[5]),
    ]
    loads[4].wait()

    def half(j, core):
        first = 2 * ((y + ORDER[j]) % 4)
        rows = pl.ds(pl.multiple_of(core * 64, 64), 64)
        left = jnp.concatenate(
            [
                jnp.concatenate([pan[l, which[first + e, l], rows] for l in range(LV)], axis=1)
                for e in range(2)
            ],
            axis=0,
        )
        return jnp.dot(left, solved[...], preferred_element_type=F32)

    for j in range(4):
        half_tx[j] = half(j, 1 - c).astype(BF)
        if j == 0:
            pl.semaphore_wait(bar, 20 if CHAIN else 23)
            if CHAIN:
                for k in (2, -2):
                    signal(near, device(y, (z + k) % NZ, c, x))
        send(half_tx.at[j], half_rx.at[j], half_s, half_r.at[j], device(y, z, 1 - c, x))
    for j in range(4):
        dy = ORDER[j]
        part = half(j, c)
        take(half_rx.at[j], half_r.at[j])
        tx1[j] = (part + half_rx[j].astype(F32)).astype(BF)
        for r in range(4):
            d = (r - z + 2) % 4
            slot = dy * 4 + d
            piece = tx1.at[j, pl.ds(r * 32, 32)]
            if dy:
                send(piece, rx1.at[slot], s1_s, s1_r, device((y + dy) % 4, (z + d - 2) % NZ, c, x))
            else:

                @pl.when(d != 2)
                def _():
                    send(piece, rx1.at[slot], s1_s, s1_r, device(y, (z + d - 2) % NZ, c, x))

                @pl.when(d == 2)
                def _():
                    rx1[2] = piece[...]

    if CHAIN:
        pl.semaphore_wait(near, 2)
        for k in (4, -4):
            signal(far, device(y, (z + k) % NZ, c, x))
    outs[0].start()
    loads[6].wait()
    if TSEND:
        for k in (2, 1, 3):
            send(tops.at[x], tops.at[x], t_s, t_r, device(y, z, c, (x + k) % 4))

    def turn(l, _):
        flip[l] = pan[l, 0:4].reshape(512, 128).T
        return 0

    def turn_inv(l, _):
        invt[l] = inv[l].T
        return 0

    lax.fori_loop(0, LV // 2, turn, 0)
    take(rx1.at[pl.ds(0, 15)], s1_r)
    total = rx1[0].astype(F32)
    for slot in range(1, 16):
        total = total + rx1[slot].astype(F32)
    tx2[...] = total.astype(BF)
    if CHAIN:
        pl.semaphore_wait(far, 2)
    for k in (2, 1, 3):
        send(tx2, rx2.at[za], s2_s, s2_r, device(y, (z + 4 * k) % NZ, c, x))
    rx2[za] = tx2[...]
    lax.fori_loop(LV // 2, LV, turn, 0)
    outs[1].start()
    lax.fori_loop(0, LV, turn_inv, 0)
    outs[2].start()
    if TSEND:
        take(tops.at[pl.ds(0, 3)], t_r)
    outs[4].start()
    for t in range(4):
        topt[t] = tops[t].T
    outs[5].start()
    loads[5].wait()
    take(rx2.at[pl.ds(0, 3)], s2_r)
    total = rx2[0].astype(F32)
    for k in range(1, 4):
        total = total + rx2[k].astype(F32)
    mine_red[...] = (trhs[...].astype(F32) - total).astype(BF)
    for dy in (2, 1, 3, 0):
        for d in (-2, 1, -1, 0):
            if (dy, d) != (0, 0):
                send(mine_red, red_o.at[c, grp], s3_s, s3_r.at[dy], device((y + dy) % 4, (z + d) % NZ, c, x))
    outs[3].start()
    outs[3].wait()
    for dy in (0, 1, 3, 2):
        from_y = (y - dy) % 4
        quarter = red_o.at[c, pl.ds(pl.multiple_of(from_y * 4, 4), 4)]
        take(red_o.at[c, pl.ds(0, 3 if dy == 0 else 4)], s3_r.at[dy])
        send(quarter, quarter, s4_s, s4_r.at[dy], device(y, z, 1 - c, x))
    take(half_tx, half_s)
    take(rx1.at[pl.ds(0, 15)], s1_s)
    take(rx2.at[pl.ds(0, 3)], s2_s)
    take(rx1.at[pl.ds(0, 15)], s3_s)
    if TSEND:
        take(tops.at[pl.ds(0, 3)], t_s)
    for k in (0, 1, 2, 4, 5):
        outs[k].wait()
    for dy in (0, 1, 3, 2):
        take(red_o.at[c, pl.ds(0, 4)], s4_r.at[dy])
    take(red_o.at[c], s4_s)


def backward_kernel(red, tops, topt, solved, flip, invt, anc_h, pat_h, out_h, x_h, known, rem, out, anc, pat, sems):
    loads = [
        pltpu.make_async_copy(anc_h, anc, sems.at[LV + 1]),
        pltpu.make_async_copy(pat_h, pat, sems.at[LV + 2]),
    ]
    for load in loads:
        load.start()
    known[pl.ds(NB, 1)] = jnp.zeros((1, 128, 128), BF)
    middles = []
    for t in range(4):
        parts = []
        for j in range(2):
            for core in range(2):
                for h in range(2):
                    parts.append(red[core, t * 4 + 2 * j + h])
        middles.append(jnp.dot(tops[t], jnp.concatenate(parts, axis=0), preferred_element_type=F32).astype(BF))
    for t in range(4):
        top = jnp.dot(topt[t], middles[t], preferred_element_type=F32).astype(BF)
        known[pl.ds(2 * t, 2)] = top.reshape(2, 128, 128)
    x_copy = pltpu.make_async_copy(known.at[pl.ds(0, NB)], x_h, sems.at[LV])
    x_copy.start()
    for load in loads:
        load.wait()
    for l in range(LV):
        parts = []
        for k in range(4):
            parts.append(known[jnp.where(pat[k, l] != 0, anc[k, l], NB)])
        back = jnp.dot(flip[l], jnp.concatenate(parts, axis=0), preferred_element_type=F32)
        rem[l] = (solved[l].astype(F32) - back).astype(BF)
    copies = []
    for l in range(LV):
        out[l] = jnp.dot(invt[l], rem[l], preferred_element_type=F32)
        if l % PER == PER - 1:
            some = pl.ds(l + 1 - PER, PER)
            copies.append(pltpu.make_async_copy(out.at[some], out_h.at[some], sems.at[l]))
            copies[-1].start()
    for copy in copies:
        copy.wait()
    x_copy.wait()


def shards(leaf_rhs, leaf_inverse, panels, ancestors, pattern, top_rhs, top_inverse):
    hbm = pl.BlockSpec(memory_space=pltpu.HBM)
    any_spec = pl.BlockSpec(memory_space=pl.ANY)
    vmem = pl.BlockSpec(memory_space=pltpu.VMEM)
    V, D = pltpu.VMEM, pltpu.SemaphoreType.DMA
    anc, pat = ancestors.T, pattern.T
    shape = jax.ShapeDtypeStruct
    solved, flip, invt, tops, topt, red = pl.pallas_call(
        forward_kernel,
        out_shape=(
            shape((2048, 128), BF), shape((LV, 128, 512), BF), shape((LV, 128, 128), BF),
            shape((4, 256, 256), BF), shape((4, 256, 256), BF), shape((2, 16, 32, 128), BF),
        ),
        in_specs=[hbm] * 7,
        out_specs=(any_spec,) * 6,
        scratch_shapes=[
            V((2048, 128), BF), V((LV, 128, 128), BF), V((LV, 5, 128, 128), BF),
            pltpu.SMEM((4, LV), jnp.int32), pltpu.SMEM((4, LV), jnp.int32), pltpu.SMEM((NB, LV), jnp.int32),
            V((2048, 128), BF), V((LV, 128, 512), BF), V((LV, 128, 128), BF), V((4, 256, 256), BF), V((4, 256, 256), BF),
            V((4, 128, 128), BF), V((4, 128, 128), BF), V((4, 128, 128), BF), V((16, 32, 128), BF),
            V((32, 128), BF), V((4, 32, 128), BF), V((32, 128), BF), V((32, 128), BF),
            D((7,)), D((6,)), pltpu.SemaphoreType.REGULAR, pltpu.SemaphoreType.REGULAR,
            D, D((4,)), D, D, D, D, D, D((4,)), D, D((4,)), D, D,
        ],
        compiler_params=pltpu.CompilerParams(collective_id=0, has_side_effects=True, vmem_limit_bytes=20 * 2**20),
        cost_estimate=pl.CostEstimate(flops=700_000_000, bytes_accessed=4_000_000, transcendentals=0),
        name="forward",
    )(*(pltpu.with_memory_space_constraint(a, pltpu.HBM) for a in (leaf_rhs, leaf_inverse, panels, anc, pat, top_rhs, top_inverse)))
    leaf_solution, top_solution = pl.pallas_call(
        backward_kernel,
        out_shape=(shape((LV, 128, 128), F32), shape((NB, 128, 128), BF)),
        in_specs=[vmem] * 6 + [any_spec] * 2,
        out_specs=(hbm, hbm),
        scratch_shapes=[
            V((NB + 1, 128, 128), BF), V((LV, 128, 128), BF), V((LV, 128, 128), F32),
            pltpu.SMEM((4, LV), jnp.int32), pltpu.SMEM((4, LV), jnp.int32), D((LV + 3,)),
        ],
        compiler_params=pltpu.CompilerParams(vmem_limit_bytes=20 * 2**20),
        cost_estimate=pl.CostEstimate(flops=400_000_000, bytes_accessed=4_000_000, transcendentals=0),
        name="backward",
    )(red, tops, topt, solved.reshape(LV, 128, 128), flip, invt, anc, pat)
    return leaf_solution.reshape(LV * 128, 128), top_solution.reshape(NB * 128, 128)


def solution(mesh):
    placed = (
        P("leaf", "rhs"),
        P("leaf", None, None),
        P("leaf", None, None, None),
        P("leaf", None),
        P("leaf", None),
        P(None, "rhs"),
        P("rhs", None, None),
    )
    return jax.shard_map(
        shards, mesh=mesh, in_specs=placed, out_specs=(P("leaf", "rhs"), P(None, "rhs")), check_vma=False
    )
```

time: 52.5 us -> 38.5 us (0.73)
  local copies, waits for them, and re-layouts: 7.05 us -> 0.01 us
  Pallas kernels: 44.4 us -> 37.7 us
    unnamed x14 -> x4, local copies, waits for them, and re-layouts: 7.05 us -> 0.01 us
    pallas_call x2, Pallas kernels: 44.4 us -> 37.7 us  [the longest x1 35.1 us: shards(): pl.pallas_call(forward_kernel, out_shape=(shape((2048, 128), BF), shape((...]
where the time goes in v2:
time: 38.5 us; the launch traced here: 38.4 us
  Pallas kernels  37.7 us (98%)
  between operations  0.67 us (2%)
    pallas_call x1, Pallas kernels, shards(): pl.pallas_call(forward_kernel, out_shape=(shape((2048, 128), BF), shape((...  35.1 us
    pallas_call x1, Pallas kernels, shards(): pl.pallas_call(backward_kernel, out_shape=(shape((LV, 128, 128), F32), sh...  2.62 us

profile of v2, /device:TPU:1, one launch (start us, length us, event | category | flops | bytes accessed | tf_op | source)
XLA Modules:
  0.0 38.4 jit_solution(7957756767265862530)
XLA Ops:
  0.6 0.0 copy-start.1
  0.6 0.0 copy-start
  0.7 35.1 %forward.1 = (bf16[2048,128]{1,0:T(8,128)(2,1)S(1)}, bf16[16,128,512]{2,1,0:T(8,128)(2,1)S(1)}, bf16[16,128,128]{2,1,0:T(8,128)(2,1)S(1)}, bf16[4,256,256]{2,1,0...) custom-call(bf16[2048,128]{1,0:T(8,128)(2,1)} %rhs_h.1, ...), custom_call_target="tpu_custom_call" | custom-call | flops 700000000 | bytes 4000000 | tf_op jit(solution)/shard_map/forward/pallas_call | solution.py:263
  35.8 0.0 copy-done.1
  35.8 0.0 copy-done
  35.8 2.6 %backward.1 = (f32[16,128,128]{2,1,0:T(8,128)}, bf16[8,128,128]{2,1,0:T(8,128)(2,1)}) custom-call(bf16[2,16,32,128]{3,2,1,0:T(8,128)(2,1)S(1)} %get-tuple-element.10.red, bf16[4,256,256]{2,1,0:T(8,128)(2,1)S(1)} %get-tuple-element.11.tops, bf16[4,256,256]{2,1,0:T(8,128)(2,1)S(1)} %get-tuple-element.12.topt, bf16[16,128,128]{2,1,0:T(8,128)(2,1)S(1)} %bitcast.5, ...), custom_call_target="tpu_custom_call" | custom-call | flops 400000000 | bytes 4000000 | tf_op jit(solution)/shard_map/backward/pallas_call | solution.py:284
Async XLA Ops:
  0.6 35.1 %copy-start.1 = (s32[16,4]{0,1:T(4,128)S(1)}, s32[16,4]{0,1:T(4,128)}, u32[]{:S(2)}) copy-start(s32[16,4]{0,1:T(4,128)} %param.11) | copy-start | bytes 772
  0.6 35.1 %copy-start = (s32[16,4]{0,1:T(4,128)S(1)}, s32[16,4]{0,1:T(4,128)}, u32[]{:S(2)}) copy-start(s32[16,4]{0,1:T(4,128)} %param.10) | copy-start | bytes 772

commit v3 on v2

v3 whole, which is shorter than its diff:
```python
import functools
import jax
import jax.numpy as jnp
from jax import lax
from jax.experimental import pallas as pl
from jax.experimental.pallas import tpu as pltpu
from jax.sharding import PartitionSpec as P

MESH = pl.DeviceIdType.MESH
BF = jnp.bfloat16
F32 = jnp.float32
NY, NZ = 4, 16
LV = 16
NB = 8
TSEND = True
ORDER = (2, 1, 3, 0)
PER = 2
SPLIT = 4


def place():
    leaf = lax.axis_index("leaf")
    return leaf // (2 * NZ), (leaf // 2) % NZ, leaf % 2, lax.axis_index("rhs")


def device(y, z, c, x):
    return ((y * NZ + z) * 2 + c, x)


def send(src, dst, send_sem, recv_sem, to):
    pltpu.make_async_remote_copy(
        src_ref=src, dst_ref=dst, send_sem=send_sem, recv_sem=recv_sem, device_id=to, device_id_type=MESH
    ).start()


def take(like, sem):
    pltpu.make_async_copy(like, like, sem).wait()


def forward_kernel(
    rhs_h, inv_h, pan_h, anc_h, pat_h, trhs_h, tinv_h, solved_o, flip_o, invt_o, tops_o, topt_o, red_o,
    rhs, inv, pan, anc, pat, which, solved, flip, invt, tops, topt,
    tx1, rx1, tx2, rx2, trhs, mine_red,
    in_sem, out_sem, near, far, s1_s, s1_r, s2_s, s2_r, s3_s, s3_r, t_s, t_r,
):
    y, z, c, x = place()
    zr, za = z % 4, z // 4
    bar = pltpu.get_barrier_semaphore()

    loads = [
        pltpu.make_async_copy(anc_h, anc, in_sem.at[0]),
        pltpu.make_async_copy(pat_h, pat, in_sem.at[1]),
        pltpu.make_async_copy(rhs_h, rhs, in_sem.at[2]),
        pltpu.make_async_copy(inv_h, inv, in_sem.at[3]),
        pltpu.make_async_copy(trhs_h.at[pl.ds(pl.multiple_of((y * 8 + c * 4 + zr) * 32, 32), 32)], trhs, in_sem.at[4]),
        pltpu.make_async_copy(tinv_h.at[0], tops.at[x], in_sem.at[5]),
    ]
    pan_loads = []
    for k in range(SPLIT):
        some = pl.ds(k * (LV // SPLIT), LV // SPLIT)
        pan_loads.append(pltpu.make_async_copy(pan_h.at[some], pan.at[some, pl.ds(0, 4)], in_sem.at[6 + k]))
    loads = loads[:4] + pan_loads + loads[4:]
    for load in loads:
        load.start()

    def signal(sem, to):
        pl.semaphore_signal(sem, inc=1, device_id=to, device_id_type=MESH)

    for dy in (2, 1, 3):
        for d in range(4):
            for core in range(2):
                signal(bar, device((y - dy) % 4, (z - (c - 2) - d) % NZ, core, x))
    for d in range(4):
        signal(bar, device(y, (z - (c - 2) - d) % NZ, 1 - c, x))
    for d in (-2, 2, -1, 1):
        signal(bar, device(y, (z + d) % NZ, c, x))
    for k in (2, 1, 3):
        signal(bar, device(y, z, c, (x + k) % 4))

    pan[:, 4] = jnp.zeros((LV, 128, 128), BF)
    for load in loads[:4]:
        load.wait()
    for l in range(LV):
        stored = [jnp.where(pat[k, l] != 0, k, 4) for k in range(4)]
        blocks = [anc[k, l] for k in range(4)]
        for b in range(NB):
            kk = 4
            for k in range(4):
                kk = jnp.where(blocks[k] == b, stored[k], kk)
            which[b, l] = kk
        rows = pl.ds(l * 128, 128)
        solved[rows] = jnp.dot(inv[l], rhs[rows], preferred_element_type=F32).astype(BF)
    outs = [
        pltpu.make_async_copy(solved, solved_o, out_sem.at[0]),
        pltpu.make_async_copy(flip, flip_o, out_sem.at[1]),
        pltpu.make_async_copy(invt, invt_o, out_sem.at[2]),
        pltpu.make_async_copy(mine_red, red_o.at[y, c * 4 + zr], out_sem.at[3]),
        pltpu.make_async_copy(tops, tops_o, out_sem.at[4]),
        pltpu.make_async_copy(topt, topt_o, out_sem.at[5]),
    ]
    for load in pan_loads:
        load.wait()

    for j, dy in enumerate(ORDER):
        left = []
        for e in range(2):
            b = 2 * ((y + dy) % 4) + e
            left.append(jnp.concatenate([pan[l, which[b, l]] for l in range(LV)], axis=1))
        tx1[j] = jnp.dot(jnp.concatenate(left, axis=0), solved[...], preferred_element_type=F32).astype(BF)
        if j == 0:
            pl.semaphore_wait(bar, 35)
            for k in (2, -2):
                signal(near, device(y, (z + k) % NZ, c, x))
        for core in range(2):
            low = core - 2
            for r in range(4):
                d = (r - z - low) % 4
                slot = (dy * 4 + d) * 2 + c
                piece = tx1.at[j, pl.ds((core * 4 + r) * 32, 32)]
                if dy:
                    send(piece, rx1.at[slot], s1_s, s1_r, device((y + dy) % 4, (z + d + low) % NZ, core, x))
                else:
                    mine = (d + low == 0) & (c == core)

                    @pl.when(jnp.logical_not(mine))
                    def _():
                        send(piece, rx1.at[slot], s1_s, s1_r, device(y, (z + d + low) % NZ, core, x))

                    @pl.when(mine)
                    def _():
                        rx1[slot] = piece[...]

    pl.semaphore_wait(near, 2)
    for k in (4, -4):
        signal(far, device(y, (z + k) % NZ, c, x))
    outs[0].start()
    loads[-1].wait()
    if TSEND:
        for k in (2, 1, 3):
            send(tops.at[x], tops.at[x], t_s, t_r, device(y, z, c, (x + k) % 4))

    def turn(l, _):
        flip[l] = pan[l, 0:4].reshape(512, 128).T
        return 0

    def turn_inv(l, _):
        invt[l] = inv[l].T
        return 0

    lax.fori_loop(0, LV // 2, turn, 0)
    take(rx1.at[pl.ds(0, 31)], s1_r)
    total = rx1[0].astype(F32)
    for slot in range(1, 32):
        total = total + rx1[slot].astype(F32)
    tx2[...] = total.astype(BF)
    pl.semaphore_wait(far, 2)
    for k in (2, 1, 3):
        send(tx2, rx2.at[za], s2_s, s2_r, device(y, (z + 4 * k) % NZ, c, x))
    rx2[za] = tx2[...]
    lax.fori_loop(LV // 2, LV, turn, 0)
    outs[1].start()
    lax.fori_loop(0, LV, turn_inv, 0)
    outs[2].start()
    if TSEND:
        take(tops.at[pl.ds(0, 3)], t_r)
    outs[4].start()
    for t in range(4):
        topt[t] = tops[t].T
    outs[5].start()
    loads[-2].wait()
    take(rx2.at[pl.ds(0, 3)], s2_r)
    total = rx2[0].astype(F32)
    for k in range(1, 4):
        total = total + rx2[k].astype(F32)
    mine_red[...] = (trhs[...].astype(F32) - total).astype(BF)
    place_red = red_o.at[y, c * 4 + zr]
    for dy in (2, 1, 3):
        for core in range(2):
            for d in (0, 3, 1, 2):
                send(mine_red, place_red, s3_s, s3_r, device((y + dy) % 4, (z + core - 2 + d) % NZ, core, x))
    for d in range(4):
        send(mine_red, place_red, s3_s, s3_r, device(y, (z - 1 - c + d) % NZ, 1 - c, x))
    for d in (4 * c - 2, 1, -1):
        send(mine_red, place_red, s3_s, s3_r, device(y, (z + d) % NZ, c, x))
    outs[3].start()
    take(rx1.at[pl.ds(0, 31)], s1_s)
    take(rx2.at[pl.ds(0, 3)], s2_s)
    if TSEND:
        take(tops.at[pl.ds(0, 3)], t_s)
    for out in outs:
        out.wait()
    take(rx1.at[pl.ds(0, 31)], s3_r)
    take(rx1.at[pl.ds(0, 31)], s3_s)


def backward_kernel(red, tops, topt, solved, flip, invt, anc_h, pat_h, out_h, x_h, known, rem, out, anc, pat, sems):
    loads = [
        pltpu.make_async_copy(anc_h, anc, sems.at[LV + 1]),
        pltpu.make_async_copy(pat_h, pat, sems.at[LV + 2]),
    ]
    for load in loads:
        load.start()
    known[pl.ds(NB, 1)] = jnp.zeros((1, 128, 128), BF)
    middles = []
    for t in range(4):
        middles.append(jnp.dot(tops[t], red[t].reshape(256, 128), preferred_element_type=F32).astype(BF))
    for t in range(4):
        top = jnp.dot(topt[t], middles[t], preferred_element_type=F32).astype(BF)
        known[pl.ds(2 * t, 2)] = top.reshape(2, 128, 128)
    x_copy = pltpu.make_async_copy(known.at[pl.ds(0, NB)], x_h, sems.at[LV])
    x_copy.start()
    for load in loads:
        load.wait()
    for l in range(LV):
        parts = []
        for k in range(4):
            parts.append(known[jnp.where(pat[k, l] != 0, anc[k, l], NB)])
        back = jnp.dot(flip[l], jnp.concatenate(parts, axis=0), preferred_element_type=F32)
        rem[l] = (solved[l].astype(F32) - back).astype(BF)
    copies = []
    for l in range(LV):
        out[l] = jnp.dot(invt[l], rem[l], preferred_element_type=F32)
        if l % PER == PER - 1:
            some = pl.ds(l + 1 - PER, PER)
            copies.append(pltpu.make_async_copy(out.at[some], out_h.at[some], sems.at[l]))
            copies[-1].start()
    for copy in copies:
        copy.wait()
    x_copy.wait()


def shards(leaf_rhs, leaf_inverse, panels, ancestors, pattern, top_rhs, top_inverse):
    hbm = pl.BlockSpec(memory_space=pltpu.HBM)
    any_spec = pl.BlockSpec(memory_space=pl.ANY)
    vmem = pl.BlockSpec(memory_space=pltpu.VMEM)
    V, D = pltpu.VMEM, pltpu.SemaphoreType.DMA
    anc, pat = ancestors.T, pattern.T
    shape = jax.ShapeDtypeStruct
    solved, flip, invt, tops, topt, red = pl.pallas_call(
        forward_kernel,
        out_shape=(
            shape((2048, 128), BF), shape((LV, 128, 512), BF), shape((LV, 128, 128), BF),
            shape((4, 256, 256), BF), shape((4, 256, 256), BF), shape((4, 8, 32, 128), BF),
        ),
        in_specs=[hbm] * 7,
        out_specs=(any_spec,) * 6,
        scratch_shapes=[
            V((2048, 128), BF), V((LV, 128, 128), BF), V((LV, 5, 128, 128), BF),
            pltpu.SMEM((4, LV), jnp.int32), pltpu.SMEM((4, LV), jnp.int32), pltpu.SMEM((NB, LV), jnp.int32),
            V((2048, 128), BF), V((LV, 128, 512), BF), V((LV, 128, 128), BF), V((4, 256, 256), BF), V((4, 256, 256), BF),
            V((4, 256, 128), BF), V((32, 32, 128), BF),
            V((32, 128), BF), V((4, 32, 128), BF), V((32, 128), BF), V((32, 128), BF),
            D((6 + SPLIT,)), D((6,)), pltpu.SemaphoreType.REGULAR, pltpu.SemaphoreType.REGULAR,
            D, D, D, D, D, D, D, D,
        ],
        compiler_params=pltpu.CompilerParams(collective_id=0, has_side_effects=True, vmem_limit_bytes=20 * 2**20),
        cost_estimate=pl.CostEstimate(flops=700_000_000, bytes_accessed=4_000_000, transcendentals=0),
        name="forward",
    )(*(pltpu.with_memory_space_constraint(a, pltpu.HBM) for a in (leaf_rhs, leaf_inverse, panels, anc, pat, top_rhs, top_inverse)))
    leaf_solution, top_solution = pl.pallas_call(
        backward_kernel,
        out_shape=(shape((LV, 128, 128), F32), shape((NB, 128, 128), BF)),
        in_specs=[vmem] * 6 + [any_spec] * 2,
        out_specs=(hbm, hbm),
        scratch_shapes=[
            V((NB + 1, 128, 128), BF), V((LV, 128, 128), BF), V((LV, 128, 128), F32),
            pltpu.SMEM((4, LV), jnp.int32), pltpu.SMEM((4, LV), jnp.int32), D((LV + 3,)),
        ],
        compiler_params=pltpu.CompilerParams(vmem_limit_bytes=20 * 2**20),
        cost_estimate=pl.CostEstimate(flops=400_000_000, bytes_accessed=4_000_000, transcendentals=0),
        name="backward",
    )(red, tops, topt, solved.reshape(LV, 128, 128), flip, invt, anc, pat)
    return leaf_solution.reshape(LV * 128, 128), top_solution.reshape(NB * 128, 128)


def solution(mesh):
    placed = (
        P("leaf", "rhs"),
        P("leaf", None, None),
        P("leaf", None, None, None),
        P("leaf", None),
        P("leaf", None),
        P(None, "rhs"),
        P("rhs", None, None),
    )
    return jax.shard_map(
        shards, mesh=mesh, in_specs=placed, out_specs=(P("leaf", "rhs"), P(None, "rhs")), check_vma=False
    )
```

time: 38.5 us -> 36.4 us (0.945)
  Pallas kernels: 37.7 us -> 35.6 us
    pallas_call x1, Pallas kernels: 35.1 us -> 32.9 us  [shards(): pl.pallas_call(forward_kernel, out_shape=(shape((2048, 128), BF), shape((...]
where the time goes in v3:
time: 36.4 us; the launch traced here: 36.2 us
  Pallas kernels  35.6 us (98%)
  between operations  0.67 us (2%)
    pallas_call x1, Pallas kernels, shards(): pl.pallas_call(forward_kernel, out_shape=(shape((2048, 128), BF), shape((...  32.9 us
    pallas_call x1, Pallas kernels, shards(): pl.pallas_call(backward_kernel, out_shape=(shape((LV, 128, 128), F32), sh...  2.61 us

profile of v3, /device:TPU:1, one launch (start us, length us, event | category | flops | bytes accessed | tf_op | source)
XLA Modules:
  0.0 36.2 jit_solution(15439377114282689883)
XLA Ops:
  0.6 0.0 copy-start.1
  0.6 0.0 copy-start
  0.7 32.9 %forward.1 = (bf16[2048,128]{1,0:T(8,128)(2,1)S(1)}, bf16[16,128,512]{2,1,0:T(8,128)(2,1)S(1)}, bf16[16,128,128]{2,1,0:T(8,128)(2,1)S(1)}, bf16[4,256,256]{2,1,0...) custom-call(bf16[2048,128]{1,0:T(8,128)(2,1)} %rhs_h.1, ...), custom_call_target="tpu_custom_call" | custom-call | flops 700000000 | bytes 4000000 | tf_op jit(solution)/shard_map/forward/pallas_call | solution.py:239
  33.6 0.0 copy-done.1
  33.6 0.0 copy-done
  33.6 2.6 %backward.1 = (f32[16,128,128]{2,1,0:T(8,128)}, bf16[8,128,128]{2,1,0:T(8,128)(2,1)}) custom-call(bf16[4,8,32,128]{3,2,1,0:T(8,128)(2,1)S(1)} %get-tuple-element.10.red, bf16[4,256,256]{2,1,0:T(8,128)(2,1)S(1)} %get-tuple-element.11.tops, bf16[4,256,256]{2,1,0:T(8,128)(2,1)S(1)} %get-tuple-element.12.topt, bf16[16,128,128]{2,1,0:T(8,128)(2,1)S(1)} %bitcast.5, ...), custom_call_target="tpu_custom_call" | custom-call | flops 400000000 | bytes 4000000 | tf_op jit(solution)/shard_map/backward/pallas_call | solution.py:260
Async XLA Ops:
  0.6 33.0 %copy-start.1 = (s32[16,4]{0,1:T(4,128)S(1)}, s32[16,4]{0,1:T(4,128)}, u32[]{:S(2)}) copy-start(s32[16,4]{0,1:T(4,128)} %param.11) | copy-start | bytes 772
  0.6 33.0 %copy-start = (s32[16,4]{0,1:T(4,128)S(1)}, s32[16,4]{0,1:T(4,128)}, u32[]{:S(2)}) copy-start(s32[16,4]{0,1:T(4,128)} %param.10) | copy-start | bytes 772

commit v4 on v3

--- a/solution.py
+++ b/solution.py
@@ -44,7 +44,8 @@
     in_sem, out_sem, near, far, s1_s, s1_r, s2_s, s2_r, s3_s, s3_r, t_s, t_r,
 ):
     y, z, c, x = place()
-    zr, za = z % 4, z // 4
+    za = z // 4
+    zc = (z + 2) % 4
     bar = pltpu.get_barrier_semaphore()
 
     loads = [
@@ -52,7 +53,7 @@
         pltpu.make_async_copy(pat_h, pat, in_sem.at[1]),
         pltpu.make_async_copy(rhs_h, rhs, in_sem.at[2]),
         pltpu.make_async_copy(inv_h, inv, in_sem.at[3]),
-        pltpu.make_async_copy(trhs_h.at[pl.ds(pl.multiple_of((y * 8 + c * 4 + zr) * 32, 32), 32)], trhs, in_sem.at[4]),
+        pltpu.make_async_copy(trhs_h.at[pl.ds(pl.multiple_of((y * 8 + c * 4 + zc) * 32, 32), 32)], trhs, in_sem.at[4]),
         pltpu.make_async_copy(tinv_h.at[0], tops.at[x], in_sem.at[5]),
     ]
     pan_loads = []
@@ -94,7 +95,7 @@
         pltpu.make_async_copy(solved, solved_o, out_sem.at[0]),
         pltpu.make_async_copy(flip, flip_o, out_sem.at[1]),
         pltpu.make_async_copy(invt, invt_o, out_sem.at[2]),
-        pltpu.make_async_copy(mine_red, red_o.at[y, c * 4 + zr], out_sem.at[3]),
+        pltpu.make_async_copy(mine_red, red_o.at[y, c * 4 + zc], out_sem.at[3]),
         pltpu.make_async_copy(tops, tops_o, out_sem.at[4]),
         pltpu.make_async_copy(topt, topt_o, out_sem.at[5]),
     ]
@@ -154,9 +155,8 @@
         total = total + rx1[slot].astype(F32)
     tx2[...] = total.astype(BF)
     pl.semaphore_wait(far, 2)
-    for k in (2, 1, 3):
-        send(tx2, rx2.at[za], s2_s, s2_r, device(y, (z + 4 * k) % NZ, c, x))
-    rx2[za] = tx2[...]
+    for k in (6, -6, 2, -2):
+        send(tx2, rx2.at[za], s2_s, s2_r, device(y, (z + k) % NZ, c, x))
     lax.fori_loop(LV // 2, LV, turn, 0)
     outs[1].start()
     lax.fori_loop(0, LV, turn_inv, 0)
@@ -168,12 +168,12 @@
         topt[t] = tops[t].T
     outs[5].start()
     loads[-2].wait()
-    take(rx2.at[pl.ds(0, 3)], s2_r)
+    take(rx2, s2_r)
     total = rx2[0].astype(F32)
     for k in range(1, 4):
         total = total + rx2[k].astype(F32)
     mine_red[...] = (trhs[...].astype(F32) - total).astype(BF)
-    place_red = red_o.at[y, c * 4 + zr]
+    place_red = red_o.at[y, c * 4 + zc]
     for dy in (2, 1, 3):
         for core in range(2):
             for d in (0, 3, 1, 2):
@@ -184,7 +184,7 @@
         send(mine_red, place_red, s3_s, s3_r, device(y, (z + d) % NZ, c, x))
     outs[3].start()
     take(rx1.at[pl.ds(0, 31)], s1_s)
-    take(rx2.at[pl.ds(0, 3)], s2_s)
+    take(rx2, s2_s)
     if TSEND:
         take(tops.at[pl.ds(0, 3)], t_s)
     for out in outs:

time: 36.4 us -> 35.7 us (0.981)
  Pallas kernels: 35.6 us -> 34.9 us
    pallas_call x1, Pallas kernels: 32.9 us -> 32.3 us  [shards(): pl.pallas_call(forward_kernel, out_shape=(shape((2048, 128), BF), shape((...]
where the time goes in v4:
time: 35.7 us; the launch traced here: 35.6 us
  Pallas kernels  34.9 us (98%)
  between operations  0.67 us (2%)
    pallas_call x1, Pallas kernels, shards(): pl.pallas_call(forward_kernel, out_shape=(shape((2048, 128), BF), shape((...  32.3 us
    pallas_call x1, Pallas kernels, shards(): pl.pallas_call(backward_kernel, out_shape=(shape((LV, 128, 128), F32), sh...  2.61 us

profile of v4, /device:TPU:1, one launch (start us, length us, event | category | flops | bytes accessed | tf_op | source)
XLA Modules:
  0.0 35.6 jit_solution(9838608250130335328)
XLA Ops:
  0.6 0.0 copy-start.1
  0.6 0.0 copy-start
  0.7 32.3 %forward.1 = (bf16[2048,128]{1,0:T(8,128)(2,1)S(1)}, bf16[16,128,512]{2,1,0:T(8,128)(2,1)S(1)}, bf16[16,128,128]{2,1,0:T(8,128)(2,1)S(1)}, bf16[4,256,256]{2,1,0...) custom-call(bf16[2048,128]{1,0:T(8,128)(2,1)} %rhs_h.1, ...), custom_call_target="tpu_custom_call" | custom-call | flops 700000000 | bytes 4000000 | tf_op jit(solution)/shard_map/forward/pallas_call | solution.py:239
  32.9 0.0 copy-done.1
  32.9 0.0 copy-done
  32.9 2.6 %backward.1 = (f32[16,128,128]{2,1,0:T(8,128)}, bf16[8,128,128]{2,1,0:T(8,128)(2,1)}) custom-call(bf16[4,8,32,128]{3,2,1,0:T(8,128)(2,1)S(1)} %get-tuple-element.10.red, bf16[4,256,256]{2,1,0:T(8,128)(2,1)S(1)} %get-tuple-element.11.tops, bf16[4,256,256]{2,1,0:T(8,128)(2,1)S(1)} %get-tuple-element.12.topt, bf16[16,128,128]{2,1,0:T(8,128)(2,1)S(1)} %bitcast.5, ...), custom_call_target="tpu_custom_call" | custom-call | flops 400000000 | bytes 4000000 | tf_op jit(solution)/shard_map/backward/pallas_call | solution.py:260
Async XLA Ops:
  0.6 32.3 %copy-start.1 = (s32[16,4]{0,1:T(4,128)S(1)}, s32[16,4]{0,1:T(4,128)}, u32[]{:S(2)}) copy-start(s32[16,4]{0,1:T(4,128)} %param.11) | copy-start | bytes 772
  0.6 32.3 %copy-start = (s32[16,4]{0,1:T(4,128)S(1)}, s32[16,4]{0,1:T(4,128)}, u32[]{:S(2)}) copy-start(s32[16,4]{0,1:T(4,128)} %param.10) | copy-start | bytes 772

commit v5 on v4

--- a/solution.py
+++ b/solution.py
@@ -112,22 +112,22 @@
             pl.semaphore_wait(bar, 35)
             for k in (2, -2):
                 signal(near, device(y, (z + k) % NZ, c, x))
-        for core in range(2):
-            low = core - 2
-            for r in range(4):
-                d = (r - z - low) % 4
+        for d in range(4):
+            for core in range(2):
+                low = core - 2
+                r = (z + low + d) % 4
                 slot = (dy * 4 + d) * 2 + c
-                piece = tx1.at[j, pl.ds((core * 4 + r) * 32, 32)]
-                if dy:
-                    send(piece, rx1.at[slot], s1_s, s1_r, device((y + dy) % 4, (z + d + low) % NZ, core, x))
+                piece = tx1.at[j, pl.ds(pl.multiple_of((core * 4 + r) * 32, 32), 32)]
+                to = device((y + dy) % 4, (z + d + low) % NZ, core, x)
+                if dy or d + low:
+                    send(piece, rx1.at[slot], s1_s, s1_r, to)
                 else:
-                    mine = (d + low == 0) & (c == core)
-
-                    @pl.when(jnp.logical_not(mine))
+
+                    @pl.when(c != core)
                     def _():
-                        send(piece, rx1.at[slot], s1_s, s1_r, device(y, (z + d + low) % NZ, core, x))
-
-                    @pl.when(mine)
+                        send(piece, rx1.at[slot], s1_s, s1_r, to)
+
+                    @pl.when(c == core)
                     def _():
                         rx1[slot] = piece[...]
 
@@ -174,14 +174,17 @@
         total = total + rx2[k].astype(F32)
     mine_red[...] = (trhs[...].astype(F32) - total).astype(BF)
     place_red = red_o.at[y, c * 4 + zc]
-    for dy in (2, 1, 3):
-        for core in range(2):
-            for d in (0, 3, 1, 2):
-                send(mine_red, place_red, s3_s, s3_r, device((y + dy) % 4, (z + core - 2 + d) % NZ, core, x))
-    for d in range(4):
-        send(mine_red, place_red, s3_s, s3_r, device(y, (z - 1 - c + d) % NZ, 1 - c, x))
-    for d in (4 * c - 2, 1, -1):
-        send(mine_red, place_red, s3_s, s3_r, device(y, (z + d) % NZ, c, x))
+    for i in range(4):
+        for up in range(4):
+            dy = (up - y) % 4
+            for core in range(2):
+                base = (z + core - 2) % NZ
+                d = (i + jnp.where(base > NZ - 4, NZ - base, 0)) % 4
+                to = device((y + dy) % 4, (base + d) % NZ, core, x)
+                @pl.when((dy != 0) | (core != c) | (d + core != 2))
+                def _():
+                    send(mine_red, place_red, s3_s, s3_r, to)
+
     outs[3].start()
     take(rx1.at[pl.ds(0, 31)], s1_s)
     take(rx2, s2_s)

time: 35.7 us -> 35.1 us (0.983)
  Pallas kernels: 34.9 us -> 34.3 us
    pallas_call x1, Pallas kernels: 32.3 us -> 31.6 us  [shards(): pl.pallas_call(forward_kernel, out_shape=(shape((2048, 128), BF), shape((...]
where the time goes in v5:
time: 35.1 us; the launch traced here: 34.9 us
  Pallas kernels  34.3 us (98%)
  between operations  0.67 us (2%)
    pallas_call x1, Pallas kernels, shards(): pl.pallas_call(forward_kernel, out_shape=(shape((2048, 128), BF), shape((...  31.6 us
    pallas_call x1, Pallas kernels, shards(): pl.pallas_call(backward_kernel, out_shape=(shape((LV, 128, 128), F32), sh...  2.62 us

profile of v5, /device:TPU:1, one launch (start us, length us, event | category | flops | bytes accessed | tf_op | source)
XLA Modules:
  0.0 34.9 jit_solution(5611314703770652314)
XLA Ops:
  0.6 0.0 copy-start.1
  0.6 0.0 copy-start
  0.7 31.6 %forward.1 = (bf16[2048,128]{1,0:T(8,128)(2,1)S(1)}, bf16[16,128,512]{2,1,0:T(8,128)(2,1)S(1)}, bf16[16,128,128]{2,1,0:T(8,128)(2,1)S(1)}, bf16[4,256,256]{2,1,0...) custom-call(bf16[2048,128]{1,0:T(8,128)(2,1)} %rhs_h.1, ...), custom_call_target="tpu_custom_call" | custom-call | flops 700000000 | bytes 4000000 | tf_op jit(solution)/shard_map/forward/pallas_call | solution.py:242
  32.3 0.0 copy-done.1
  32.3 0.0 copy-done
  32.3 2.6 %backward.1 = (f32[16,128,128]{2,1,0:T(8,128)}, bf16[8,128,128]{2,1,0:T(8,128)(2,1)}) custom-call(bf16[4,8,32,128]{3,2,1,0:T(8,128)(2,1)S(1)} %get-tuple-element.10.red, bf16[4,256,256]{2,1,0:T(8,128)(2,1)S(1)} %get-tuple-element.11.tops, bf16[4,256,256]{2,1,0:T(8,128)(2,1)S(1)} %get-tuple-element.12.topt, bf16[16,128,128]{2,1,0:T(8,128)(2,1)S(1)} %bitcast.5, ...), custom_call_target="tpu_custom_call" | custom-call | flops 400000000 | bytes 4000000 | tf_op jit(solution)/shard_map/backward/pallas_call | solution.py:263
Async XLA Ops:
  0.6 31.7 %copy-start.1 = (s32[16,4]{0,1:T(4,128)S(1)}, s32[16,4]{0,1:T(4,128)}, u32[]{:S(2)}) copy-start(s32[16,4]{0,1:T(4,128)} %param.11) | copy-start | bytes 772
  0.6 31.7 %copy-start = (s32[16,4]{0,1:T(4,128)S(1)}, s32[16,4]{0,1:T(4,128)}, u32[]{:S(2)}) copy-start(s32[16,4]{0,1:T(4,128)} %param.10) | copy-start | bytes 772

commit v6 on v5

--- a/solution.py
+++ b/solution.py
@@ -15,6 +15,7 @@
 TSEND = True
 ORDER = (2, 1, 3, 0)
 PER = 2
+AHEAD = 1
 SPLIT = 4
 
 
@@ -102,16 +103,14 @@
     for load in pan_loads:
         load.wait()
 
-    for j, dy in enumerate(ORDER):
+    def multiply(j, dy):
         left = []
         for e in range(2):
             b = 2 * ((y + dy) % 4) + e
             left.append(jnp.concatenate([pan[l, which[b, l]] for l in range(LV)], axis=1))
         tx1[j] = jnp.dot(jnp.concatenate(left, axis=0), solved[...], preferred_element_type=F32).astype(BF)
-        if j == 0:
-            pl.semaphore_wait(bar, 35)
-            for k in (2, -2):
-                signal(near, device(y, (z + k) % NZ, c, x))
+
+    def spread(j, dy):
         for d in range(4):
             for core in range(2):
                 low = core - 2
@@ -131,8 +130,19 @@
                     def _():
                         rx1[slot] = piece[...]
 
+    for j, dy in enumerate(ORDER):
+        multiply(j, dy)
+        if j == AHEAD:
+            pl.semaphore_wait(bar, 35)
+            for k in (2, -2):
+                signal(near, device(y, (z + k) % NZ, c, x))
+            for e in range(AHEAD):
+                spread(e, ORDER[e])
+        if j >= AHEAD:
+            spread(j, dy)
+
     pl.semaphore_wait(near, 2)
-    for k in (4, -4):
+    for k in (2, -2):
         signal(far, device(y, (z + k) % NZ, c, x))
     outs[0].start()
     loads[-1].wait()
@@ -177,7 +187,7 @@
     for i in range(4):
         for up in range(4):
             dy = (up - y) % 4
-            for core in range(2):
+            for core in (1, 0):
                 base = (z + core - 2) % NZ
                 d = (i + jnp.where(base > NZ - 4, NZ - base, 0)) % 4
                 to = device((y + dy) % 4, (base + d) % NZ, core, x)

time: 35.1 us -> 35 us (level)
  no operation moved by 1% of the time
where the time goes in v6:
time: 35 us; the launch traced here: 34.9 us
  Pallas kernels  34.2 us (98%)
  between operations  0.67 us (2%)
    pallas_call x1, Pallas kernels, shards(): pl.pallas_call(forward_kernel, out_shape=(shape((2048, 128), BF), shape((...  31.6 us
    pallas_call x1, Pallas kernels, shards(): pl.pallas_call(backward_kernel, out_shape=(shape((LV, 128, 128), F32), sh...  2.61 us

profile of v6, /device:TPU:1, one launch (start us, length us, event | category | flops | bytes accessed | tf_op | source)
XLA Modules:
  0.0 34.9 jit_solution(12100812135510654871)
XLA Ops:
  0.6 0.0 copy-start.1
  0.6 0.0 copy-start
  0.7 31.6 %forward.1 = (bf16[2048,128]{1,0:T(8,128)(2,1)S(1)}, bf16[16,128,512]{2,1,0:T(8,128)(2,1)S(1)}, bf16[16,128,128]{2,1,0:T(8,128)(2,1)S(1)}, bf16[4,256,256]{2,1,0...) custom-call(bf16[2048,128]{1,0:T(8,128)(2,1)} %rhs_h.1, ...), custom_call_target="tpu_custom_call" | custom-call | flops 700000000 | bytes 4000000 | tf_op jit(solution)/shard_map/forward/pallas_call | solution.py:252
  32.3 0.0 copy-done.1
  32.3 0.0 copy-done
  32.3 2.6 %backward.1 = (f32[16,128,128]{2,1,0:T(8,128)}, bf16[8,128,128]{2,1,0:T(8,128)(2,1)}) custom-call(bf16[4,8,32,128]{3,2,1,0:T(8,128)(2,1)S(1)} %get-tuple-element.10.red, bf16[4,256,256]{2,1,0:T(8,128)(2,1)S(1)} %get-tuple-element.11.tops, bf16[4,256,256]{2,1,0:T(8,128)(2,1)S(1)} %get-tuple-element.12.topt, bf16[16,128,128]{2,1,0:T(8,128)(2,1)S(1)} %bitcast.5, ...), custom_call_target="tpu_custom_call" | custom-call | flops 400000000 | bytes 4000000 | tf_op jit(solution)/shard_map/backward/pallas_call | solution.py:273
Async XLA Ops:
  0.6 31.6 %copy-start.1 = (s32[16,4]{0,1:T(4,128)S(1)}, s32[16,4]{0,1:T(4,128)}, u32[]{:S(2)}) copy-start(s32[16,4]{0,1:T(4,128)} %param.11) | copy-start | bytes 772
  0.6 31.6 %copy-start = (s32[16,4]{0,1:T(4,128)S(1)}, s32[16,4]{0,1:T(4,128)}, u32[]{:S(2)}) copy-start(s32[16,4]{0,1:T(4,128)} %param.10) | copy-start | bytes 772
